TPU v7x, 32 devices: a whole 2x2x4 slice. The times are simulated.
32 devices in a mesh: groups: 2 (over x), tensor: 16 (over z, y, core).
Axes of the slice: x: 2, y: 2, z: 4, core: 2. Of those that a mesh axis runs over, the one named last changes fastest.
Arguments:
- tokens: bfloat16 [64, 6144], P(('groups', 'tensor')), parts along dimension 0, may hold values from -6 to 6
- attn_gain: float32 [6144], replicated, may hold values from 0.25 to 1.75
- w_qkv: bfloat16 [6144, 8192], P(None, 'tensor'), may hold values from -4 to 4
- w_out: bfloat16 [6144, 6144], P(None, 'tensor'), may hold values from -0.078125 to 0.078125
- moe_gain: float32 [6144], replicated, may hold values from 0.25 to 1.75
- w_gate: bfloat16 [6144, 4096], P(None, 'tensor'), may hold values from -0.078125 to 0.078125
- w_up: bfloat16 [6144, 4096], P(None, 'tensor'), may hold values from -0.078125 to 0.078125
- w_down: bfloat16 [4096, 6144], P('tensor'), may hold values from -0.125 to 0.125
- expert_ids: int32 [64, 2], P(('groups', 'tensor')), parts along dimension 0, may hold values from 0 to 7, as said below
- gate_weights: float32 [64, 2], P(('groups', 'tensor')), parts along dimension 0, may hold values from 0.1 to 1
Outputs:
- layer_out: bfloat16 [64, 6144], P(('groups', 'tensor')), parts along dimension 0
There are 2 independent parts, one for each index of `groups`. A program takes and returns all parts, laid end to end along the dimension named above; an argument that names none is the same for every part. Nothing has to cross between parts.
Inputs may be any that keep to these rules, and one draw needn't show every extreme that they name: `expert_ids`: each row names two different experts; in some aligned block of 2 rows every token names expert 0.
All inputs are finite; a program needn't handle non-finite values.
Results may differ from a plain program's by a relative error of at most 0.008.
Values may be sent and summed in bfloat16 or wider, within the bound.
A program may use at most 64 MiB of HBM per device.

v0:
```python
import jax
import jax.numpy as jnp
from jax import lax
from jax.sharding import PartitionSpec as P

HEADS = 48
KV_HEADS = 8
HEAD_DIM = 128
EXPERT_WINDOW = 2


def rms_scale(values, gain):
    mean_square = jnp.mean(values * values, axis=-1, keepdims=True)
    return values * lax.rsqrt(mean_square + 1e-05) * gain


def rotate(heads, positions):
    half = heads.shape[-1] // 2
    inverse = 1000000.0 ** (-(jnp.arange(half, dtype=jnp.float32) * 2.0) / heads.shape[-1])
    angles = positions[:, None] * inverse[None, :]
    cosine = jnp.cos(angles)[:, None, :]
    sine = jnp.sin(angles)[:, None, :]
    first = heads[..., :half]
    second = heads[..., half:]
    return jnp.concatenate(
        [first * cosine - second * sine, second * cosine + first * sine], axis=-1
    )


def expert_block(slots, w_gate, w_up, w_down):
    gate_part = jnp.dot(slots, w_gate, preferred_element_type=jnp.float32)
    up_part = jnp.dot(slots, w_up, preferred_element_type=jnp.float32)
    hidden = (jax.nn.silu(gate_part) * up_part).astype(jnp.bfloat16)
    return jnp.dot(hidden, w_down, preferred_element_type=jnp.float32).astype(jnp.bfloat16)


def on_device(
    tokens, attn_gain, w_qkv, w_out, moe_gain, w_gate, w_up, w_down, expert_ids, gate_weights
):
    count = lax.axis_size("tensor")
    rank = lax.axis_index("tensor")
    rows = tokens.shape[0]
    group = HEADS // KV_HEADS
    kv_width = KV_HEADS * HEAD_DIM
    att_width = HEADS * HEAD_DIM
    tok_float = tokens.astype(jnp.float32)
    normed = rms_scale(tok_float, attn_gain).astype(jnp.bfloat16)
    columns = jnp.dot(
        lax.all_gather(normed, "tensor", axis=0, tiled=True),
        w_qkv,
        preferred_element_type=jnp.float32,
    ).astype(jnp.bfloat16)
    positions = (rank * rows + jnp.arange(rows, dtype=jnp.int32)).astype(jnp.float32)
    scale = 1.0 / jnp.sqrt(jnp.float32(HEAD_DIM))
    own_qkv = lax.all_to_all(columns, "tensor", split_axis=0, concat_axis=1, tiled=True)
    queries = own_qkv[:, :att_width].reshape(rows, HEADS, HEAD_DIM).astype(jnp.float32)
    queries = rotate(queries, positions).astype(jnp.bfloat16)
    grouped = queries.reshape(rows, KV_HEADS, group, HEAD_DIM)
    size = own_qkv.shape[0]
    keys = (
        own_qkv[:, att_width : att_width + kv_width]
        .reshape(size, KV_HEADS, HEAD_DIM)
        .astype(jnp.float32)
    )
    values = own_qkv[:, att_width + kv_width :].reshape(size, KV_HEADS, HEAD_DIM)
    keys, values = (rotate(keys, positions).astype(jnp.bfloat16), values)
    running = jnp.full((KV_HEADS, group, rows), -1e30, jnp.float32)
    key_piece = lax.all_gather(keys, "tensor", axis=0, tiled=True)
    value_piece = lax.all_gather(values, "tensor", axis=0, tiled=True)
    size = key_piece.shape[0]
    router_scores = (
        jnp.einsum("qkgd,skd->kgqs", grouped, key_piece, preferred_element_type=jnp.float32) * scale
    )
    key_pos = jnp.arange(size, dtype=jnp.int32).astype(jnp.float32)
    allowed = key_pos[None, :] <= positions[:, None]
    router_scores = jnp.where(allowed, router_scores, -1e30)
    fresh = jnp.maximum(running, jnp.max(router_scores, axis=-1))
    weights = jnp.where(allowed, jnp.exp(router_scores - fresh[..., None]), 0.0)
    running_total = jnp.sum(weights, axis=-1)
    accum = jnp.einsum(
        "kgqs,skd->kgqd",
        weights.astype(jnp.bfloat16),
        value_piece,
        preferred_element_type=jnp.float32,
    )
    running, running_total, accum = (fresh, running_total, accum)
    mixed = accum / running_total[..., None]
    mixed = jnp.transpose(mixed, (2, 0, 1, 3)).reshape(rows, att_width).astype(jnp.bfloat16)
    out_columns = jnp.dot(
        lax.all_gather(mixed, "tensor", axis=0, tiled=True),
        w_out,
        preferred_element_type=jnp.float32,
    ).astype(jnp.bfloat16)
    attended = lax.all_to_all(out_columns, "tensor", split_axis=0, concat_axis=1, tiled=True)
    residual = tok_float + attended.astype(jnp.float32)
    moe_in = rms_scale(residual, moe_gain).astype(jnp.bfloat16)
    owners = count // EXPERT_WINDOW
    my_expert = rank // owners
    all_inputs = lax.all_gather(moe_in, "tensor", axis=0, tiled=True)
    all_ids, all_gates = (
        lax.all_gather(expert_ids.astype(jnp.float32), "tensor", axis=0, tiled=True),
        lax.all_gather(gate_weights, "tensor", axis=0, tiled=True),
    )
    matches = all_ids.astype(jnp.int32) == my_expert
    picked = jnp.sum(jnp.where(matches, all_gates, 0.0), axis=1)
    part = expert_block(all_inputs, w_gate, w_up, w_down)
    part_slice = part.astype(jnp.float32)
    combined = lax.psum_scatter(
        picked[:, None] * part_slice, "tensor", scatter_dimension=0, tiled=True
    )
    return (residual + combined).astype(jnp.bfloat16)


def solution(mesh):
    return jax.shard_map(
        on_device,
        mesh=mesh,
        in_specs=(
            P(("groups", "tensor"), None),
            P(),
            P(None, "tensor"),
            P(None, "tensor"),
            P(),
            P(None, "tensor"),
            P(None, "tensor"),
            P("tensor", None),
            P(("groups", "tensor"), None),
            P(("groups", "tensor"), None),
        ),
        out_specs=P(("groups", "tensor"), None),
        check_vma=False,
    )
```

profile of v0, /device:TPU:0, one launch (start us, length us, event | category | flops | bytes accessed | tf_op | source)
XLA Modules:
  0.0 284.4 jit_solution(16510092602387429996)
XLA Ops:
  6.5 0.0 copy-start
  6.5 1.1 fusion.11
  7.6 0.9 fusion.28
  8.5 24.2 %all-gather = bf16[16,2,6144]{2,1,0:T(2,128)(2,1)S(1)} all-gather(bf16[1,2,6144]{2,1,0:T(2,128)(2,1)S(1)} %fusion.28), channel_id=1, replica_groups=mesh['groups'=2,'tensor'=16] {'tensor'}, dimensions={0}, use_global_device_ids=true | all-gather | bytes 417792 | tf_op jit(solution)/shard_map/all_gather | solution.py:49
  32.6 0.9 reshape.115
  33.5 4.1 %convolution_convert_fusion.1 = bf16[32,512]{1,0:T(8,128)(2,1)S(1)} fusion(bf16[32,6144]{1,0:T(8,128)(2,1)} %reshape.115, bf16[6144,512]{1,0:T(8,128)(2,1)} %param.12), kind=kOutput, calls=%fused_computation.9 | convolution fusion | flops 201342976 | bytes 6717440 | tf_op jit(solution)/shard_map/dot_general | solution.py:48
  37.6 0.6 all_to_all.24
  38.3 3.5 %all-to-all-start = ((bf16[16,2,512]{2,1,0:T(2,128)(2,1)}), bf16[16,2,512]{2,1,0:T(2,128)(2,1)S(1)}, u32[]{:S(2)}, u32[]{:S(2)}) async-start(bf16[16,2,512]{2,1,0:T(2,128)(2,1)} %all_to_all.24), calls=%async_computation | async-start | bytes 65536 | tf_op jit(solution)/shard_map/all_to_all | solution.py:55
  41.8 0.0 copy-done.6
  41.8 0.1 multiply_cosine_fusion
  42.0 0.1 broadcast_compare_fusion
  42.0 21.7 %all-gather.2 = f32[16,2,2]{2,1,0:T(2,128)S(1)} all-gather(f32[1,2,2]{2,1,0:T(2,128)S(1)} %convert_bitcast_fusion.1), channel_id=1, replica_groups=mesh['groups'=2,'tensor'=16] {'tensor'}, dimensions={0}, use_global_device_ids=true | all-gather | bytes 272 | tf_op jit(solution)/shard_map/all_gather | solution.py:101
  63.7 0.0 copy-done.5
  63.7 18.8 %all-gather.3 = f32[16,2,2]{2,1,0:T(2,128)} all-gather(f32[1,2,2]{2,1,0:T(2,128)S(1)} %bitcast.65), channel_id=1, replica_groups=mesh['groups'=2,'tensor'=16] {'tensor'}, dimensions={0}, use_global_device_ids=true | all-gather | bytes 272 | tf_op jit(solution)/shard_map/all_gather | solution.py:102
  82.5 0.0 all-to-all-done
  82.6 0.1 subtract_convert_fusion.1
  82.6 0.1 pad_maximum_fusion
  82.7 18.9 %all_gather.22 = bf16[32,8,128]{2,1,0:T(8,128)(2,1)S(1)} all-gather(bf16[2,8,128]{2,1,0:T(8,128)(2,1)S(1)} %pad_maximum_fusion), channel_id=1, replica_groups=mesh['groups'=2,'tensor'=16] {'tensor'}, dimensions={0}, use_global_device_ids=true | all-gather | bytes 69632 | tf_op jit(solution)/shard_map/all_gather | solution.py:68
  101.7 0.1 subtract_convert_fusion
  101.8 0.3 fusion.35
  102.2 17.6 %all_gather.23 = bf16[32,8,128]{2,1,0:T(8,128)(2,1)S(1)} all-gather(bf16[2,8,128]{2,1,0:T(8,128)(2,1)S(1)} %bitcast.63), channel_id=1, replica_groups=mesh['groups'=2,'tensor'=16] {'tensor'}, dimensions={0}, use_global_device_ids=true | all-gather | bytes 69632 | tf_op jit(solution)/shard_map/all_gather | solution.py:69
  119.8 0.2 fusion.9
  119.9 0.2 fusion.5
  120.2 0.6 reshape.116
  120.8 20.1 %all-gather.1 = bf16[16,2,6144]{2,1,0:T(2,128)(2,1)S(1)} all-gather(bf16[1,2,6144]{2,1,0:T(2,128)(2,1)} %reshape.116), channel_id=1, replica_groups=mesh['groups'=2,'tensor'=16] {'tensor'}, dimensions={0}, use_global_device_ids=true | all-gather | bytes 417792 | tf_op jit(solution)/shard_map/all_gather | solution.py:90
  140.9 0.9 reshape.117
  141.8 3.2 %convolution_convert_fusion.2 = bf16[32,384]{1,0:T(8,128)(2,1)S(1)} fusion(bf16[32,6144]{1,0:T(8,128)(2,1)} %reshape.117, bf16[6144,384]{1,0:T(8,128)(2,1)} %param.13), kind=kOutput, calls=%fused_computation.10 | convolution fusion | flops 151007232 | bytes 5136384 | tf_op jit(solution)/shard_map/dot_general | solution.py:89
  145.1 0.6 all_to_all.28
  145.7 3.5 %all-to-all-start.1 = ((bf16[16,2,384]{2,1,0:T(2,128)(2,1)}), bf16[16,2,384]{2,1,0:T(2,128)(2,1)S(1)}, u32[]{:S(2)}, u32[]{:S(2)}) async-start(bf16[16,2,384]{2,1,0:T(2,128)(2,1)} %all_to_all.28), calls=%async_computation.1 | async-start | bytes 49152 | tf_op jit(solution)/shard_map/all_to_all | solution.py:94
  149.2 0.0 all-reduce.3.cloned.1.call-start
  149.2 0.0 copy-done.3
  149.2 0.1 fusion.30
  149.3 0.1 reshape.130
  149.4 6.3 %all-to-all-done.1 = bf16[16,2,384]{2,1,0:T(2,128)(2,1)S(1)} async-done(((bf16[16,2,384]{2,1,0:T(2,128)(2,1)}), bf16[16,2,384]{2,1,0:T(2,128)(2,1)S(1)}, u32[]{:S(2)}, u32[]{:S(2)}) %all-to-all-start.1) | async-done | bytes 24608 | tf_op jit(solution)/shard_map/all_to_all | solution.py:94
  155.7 0.0 copy-start.1
  155.7 0.0 copy-done.2
  155.8 0.2 multiply_reduce_fusion
  155.9 0.1 fusion.29
  156.0 0.3 copy-done.1
  156.3 20.1 %all-gather.4 = bf16[16,2,6144]{2,1,0:T(2,128)(2,1)} all-gather(bf16[1,2,6144]{2,1,0:T(2,128)(2,1)S(1)} %fusion.29), channel_id=1, replica_groups=mesh['groups'=2,'tensor'=16] {'tensor'}, dimensions={0}, use_global_device_ids=true | all-gather | bytes 417792 | tf_op jit(solution)/shard_map/all_gather | solution.py:99
  176.4 1.1 reshape.123
  177.6 3.1 %fusion.36 = f32[32,256]{1,0:T(8,128)} fusion(bf16[32,6144]{1,0:T(8,128)(2,1)S(1)} %reshape.123, bf16[6144,256]{1,0:T(8,128)(2,1)} %param.15), kind=kOutput, calls=%fused_computation.69 | convolution fusion | flops 100663296 | bytes 3571712 | tf_op jit(solution)/shard_map/dot_general | solution.py:31
  180.7 0.0 copy-done
  180.7 4.6 %fusion.1 = f32[32,6144]{1,0:T(8,128)} fusion(bf16[256,6144]{1,0:T(8,128)(2,1)S(1)} %copy-done, bf16[32,6144]{1,0:T(8,128)(2,1)S(1)} %reshape.123, bf16[6144,256]{1,0:T(8,128)(2,1)} %param.16, f32[32]{0:T(128)S(1)} %reshape.130, f32[32,256]{1,0:T(8,128)} %fusion.36), kind=kOutput, calls=%fused_computation.2 | convolution fusion | flops 201965568 | bytes 7504000 | tf_op jit(solution)/shard_map/dot_general | solution.py:34
  185.4 0.0 all-reduce.3.cloned.1.call-update
  185.4 0.6 dynamic-slice
  186.6 89.3 %all-reduce.3.cloned.1.call-done = f32[32,6144]{1,0:T(8,128)} async-done(((f32[32,6144]{1,0:T(8,128)}), f32[32,6144]{1,0:T(8,128)}) %all-reduce.3.cloned.1.call-update) | async-done | bytes 786448
  275.9 1.6 fusion.14
  (23 shorter events, 0.1 us)
Async XLA Ops:
  6.5 174.2 %copy-start = (bf16[256,6144]{1,0:T(8,128)(2,1)S(1)}, bf16[256,6144]{1,0:T(8,128)(2,1)}, u32[]{:S(2)}) copy-start(bf16[256,6144]{1,0:T(8,128)(2,1)} %param.17) | copy-start | bytes 9437188
  33.5 8.3 %copy-start.6 = (s32[2,2]{1,0:T(2,128)S(1)}, s32[2,2]{1,0:T(2,128)}, u32[]{:S(2)}) copy-start(s32[2,2]{1,0:T(2,128)} %param.18) | copy-start | bytes 52
  33.5 30.2 %copy-start.5 = (f32[2,2]{1,0:T(2,128)S(1)}, f32[2,2]{1,0:T(2,128)}, u32[]{:S(2)}) copy-start(f32[2,2]{1,0:T(2,128)} %param.19) | copy-start | bytes 52
  38.3 44.2 %all-to-all-start = ((bf16[16,2,512]{2,1,0:T(2,128)(2,1)}), bf16[16,2,512]{2,1,0:T(2,128)(2,1)S(1)}, u32[]{:S(2)}, u32[]{:S(2)}) async-start(bf16[16,2,512]{2,1,0:T(2,128)(2,1)} %all_to_all.24), calls=%async_computation | async-start | bytes 65536 | tf_op jit(solution)/shard_map/all_to_all | solution.py:55
  141.8 7.4 %copy-start.3 = (f32[16,2,2]{2,1,0:T(2,128)S(1)}, f32[16,2,2]{2,1,0:T(2,128)}, u32[]{:S(2)}) copy-start(f32[16,2,2]{2,1,0:T(2,128)} %all-gather.3) | copy-start | bytes 772
  141.8 13.9 %copy-start.2 = (bf16[2,6144]{1,0:T(2,128)(2,1)S(1)}, bf16[2,6144]{1,0:T(2,128)(2,1)}, u32[]{:S(2)}) copy-start(bf16[2,6144]{1,0:T(2,128)(2,1)} %param.10) | copy-start | bytes 73732
  141.8 14.1 %copy-start.4 = (f32[6144]{0:T(1024)S(1)}, f32[6144]{0:T(1024)}, u32[]{:S(2)}) copy-start(f32[6144]{0:T(1024)} %param.14) | copy-start | bytes 73732
  145.7 10.0 %all-to-all-start.1 = ((bf16[16,2,384]{2,1,0:T(2,128)(2,1)}), bf16[16,2,384]{2,1,0:T(2,128)(2,1)S(1)}, u32[]{:S(2)}, u32[]{:S(2)}) async-start(bf16[16,2,384]{2,1,0:T(2,128)(2,1)} %all_to_all.28), calls=%async_computation.1 | async-start | bytes 49152 | tf_op jit(solution)/shard_map/all_to_all | solution.py:94
  149.2 126.7 %all-reduce.3.cloned.1.call-start = ((), (), s32[]{:S(2)}) async-start(), calls=%async_computation.2 | async-start | bytes 1572864
  155.7 0.6 copy-start.1
  180.7 4.7 %copy-start.7 = (u32[32]{0:T(128)S(1)}, u32[32]{0:T(128)}, u32[]{:S(2)}) copy-start(u32[32]{0:T(128)} %constant.52) | copy-start | bytes 388
Sparse Core Ops, SparseCore 0:
  185.5 90.3 all-reduce.2
where the time goes:
time: 285 us; the launch traced here: 284 us
  blocking collectives  141 us (49%)
  waiting for transfers between devices  95.6 us (34%)
  matrix products  15.7 us (6%)
  between operations  14.3 us (5%)
  starting transfers between devices  7.02 us (2%)
  local copies, waits for them, and re-layouts  5.88 us (2%)
  other arithmetic  4.6 us (2%)
    unnamed x2, waiting for transfers between devices  89.3 us
    all_gather x1, blocking collectives, on_device(): lax.all_gather(normed, 'tensor', axis=0, tiled=True)  24.2 us
    all_gather x1, blocking collectives, on_device(): lax.all_gather(expert_ids.astype(jnp.float32), 'tensor', axis=0, tiled=True)  21.7 us
    all_gather x1, blocking collectives, on_device(): all_inputs = lax.all_gather(moe_in, 'tensor', axis=0, tiled=True)  20.1 us
    all_gather x1, blocking collectives, on_device(): lax.all_gather(mixed, 'tensor', axis=0, tiled=True)  20.1 us
    all_gather x1, blocking collectives, on_device(): key_piece = lax.all_gather(keys, 'tensor', axis=0, tiled=True)  18.9 us
    all_gather x1, blocking collectives, on_device(): lax.all_gather(gate_weights, 'tensor', axis=0, tiled=True)  18.8 us
    all_gather x1, blocking collectives, on_device(): value_piece = lax.all_gather(values, 'tensor', axis=0, tiled=True)  17.6 us
  transfers between devices with their start and end apart: 3, of which 2 were waited for; matrix products, arithmetic and copies ran while one was open for 0% of the time, Pallas kernels for 0%

commit v1 on v0

v1 whole, which is shorter than its diff:
```python
import functools

import jax
import jax.numpy as jnp
import numpy as np
from jax import lax
from jax.experimental import pallas as pl
from jax.experimental.pallas import tpu as pltpu
from jax.sharding import PartitionSpec as P

HEADS = 48
KV_HEADS = 8
GROUP = HEADS // KV_HEADS
HEAD_DIM = 128
EXPERT_WINDOW = 2
LANES = 128
CHUNK = 768
MESH = pl.DeviceIdType.MESH


def rotation_tables(size):
    half = HEAD_DIM // 2
    inverse = np.float32(1000000.0) ** (-(np.arange(half, dtype=np.float32) * 2.0) / HEAD_DIM)
    angles = np.arange(size, dtype=np.float32)[:, None] * inverse.astype(np.float32)[None, :]
    cosine, sine = np.cos(angles), np.sin(angles)
    return (
        np.concatenate([cosine, cosine], axis=1).astype(np.float32),
        np.concatenate([-sine, sine], axis=1).astype(np.float32),
    )


def rotate(head, cosine, sine):
    half = HEAD_DIM // 2
    swapped = jnp.concatenate([head[:, half:], head[:, :half]], axis=1)
    return head * cosine + swapped * sine


def kernel(
    n, tok_in, attn_gain_in, w_qkv_in, w_out_in, moe_gain_in, w_gate_in, w_up_in, w_down_in,
    cos_in, sin_in, ids, gates, out,
    w_qkv, w_out, w_gate, w_up, w_down, own_tok, attn_gain, moe_gain, cos_tab, sin_tab,
    stage, tok_all, tok_f32, x_all, columns, heads_out, k_buf, v_buf, mix_all, att_own, att_all,
    res_all, part_f32, part_all, part_in, small_sem, weight_sem, send_sem, recv_sem, kv_send, kv_recv,
):
    me = lax.axis_index("tensor")
    size = x_all.shape[1]
    width = x_all.shape[0] * CHUNK
    tiles = width // LANES
    rows = stage.shape[0] // tiles
    block = rows * tiles
    per_dev = w_qkv.shape[1] // HEAD_DIM
    q_devs = HEADS // per_dev
    kv_devs = KV_HEADS // per_dev
    chunks = width // CHUNK
    per_chunk = CHUNK // LANES
    out_cols = w_out.shape[1]

    small = [
        pltpu.make_async_copy(src, dst, small_sem.at[i])
        for i, (src, dst) in enumerate(
            [(tok_in, own_tok), (attn_gain_in, attn_gain), (moe_gain_in, moe_gain),
             (cos_in, cos_tab), (sin_in, sin_tab)]
        )
    ]
    weight = [
        pltpu.make_async_copy(src, dst, weight_sem.at[i])
        for i, (src, dst) in enumerate(
            [(w_qkv_in, w_qkv), (w_out_in, w_out), (w_gate_in, w_gate), (w_up_in, w_up),
             (w_down_in, w_down)]
        )
    ]
    for copy in small:
        copy.start()
    for copy in weight:
        copy.start()

    def peer(distance):
        return lax.rem(me + distance, n)

    barrier = pltpu.get_barrier_semaphore()

    @pl.loop(1, n)
    def _(distance):
        pl.semaphore_signal(
            barrier, inc=1, device_id={"tensor": peer(distance)}, device_id_type=MESH
        )

    small[0].wait()
    for tile in range(tiles):
        piece = own_tok[:, tile * LANES : (tile + 1) * LANES].astype(jnp.float32)
        for row in range(rows):
            stage[row * tiles + tile : row * tiles + tile + 1, :] = piece[row : row + 1, :]
    my_block = pl.ds(pl.multiple_of(me * block, 16), block)
    tok_all[my_block, :] = stage[...].astype(jnp.bfloat16)
    pl.semaphore_wait(barrier, n - 1)

    def remote(phase, src, dst, target):
        return pltpu.make_async_remote_copy(
            src_ref=src, dst_ref=dst, send_sem=send_sem.at[phase, target],
            recv_sem=recv_sem.at[phase, me], device_id={"tensor": target}, device_id_type=MESH,
        )

    def arrived(phase, source, dst):
        pltpu.make_async_remote_copy(
            src_ref=dst, dst_ref=dst, send_sem=send_sem.at[phase, source],
            recv_sem=recv_sem.at[phase, source], device_id={"tensor": source}, device_id_type=MESH,
        ).wait_recv()

    def token_block(ref, index):
        return ref.at[pl.ds(pl.multiple_of(index * block, 16), block), :]

    @pl.loop(1, n)
    def _(distance):
        remote(0, token_block(tok_all, me), token_block(tok_all, me), peer(distance)).start()

    @pl.loop(1, n)
    def _(distance):
        source = lax.rem(me + n - distance, n)
        arrived(0, source, token_block(tok_all, source))

    tok_f32[...] = tok_all[...].astype(jnp.float32)
    for copy in small[1:]:
        copy.wait()

    def tok_tile(tile):
        return tok_f32[pl.ds(tile, size, stride=tiles), :]

    def square_sum(chunk, total):
        for i in range(per_chunk):
            value = tok_tile(chunk * per_chunk + i)
            total = total + value * value
        return total

    total = lax.fori_loop(0, chunks, square_sum, jnp.zeros((size, LANES), jnp.float32))
    scale = lax.rsqrt(jnp.sum(total, axis=1, keepdims=True) / width + 1e-05)

    weight[0].wait()

    def project(chunk, total):
        pieces = []
        for i in range(per_chunk):
            tile = chunk * per_chunk + i
            pieces.append((tok_tile(tile) * scale * attn_gain[pl.ds(tile, 1), :]).astype(jnp.bfloat16))
        here = pl.ds(pl.multiple_of(chunk * CHUNK, CHUNK), CHUNK)
        return total + jnp.dot(
            jnp.concatenate(pieces, axis=1), w_qkv[here, :], preferred_element_type=jnp.float32
        )

    columns[...] = lax.fori_loop(
        0, chunks, project, jnp.zeros((size, w_qkv.shape[1]), jnp.float32)
    ).astype(jnp.bfloat16)

    is_query = me < q_devs
    is_key = jnp.logical_and(me >= q_devs, me < q_devs + kv_devs)
    is_value = me >= q_devs + kv_devs

    @pl.when(is_value)
    def _():
        for i in range(per_dev):
            heads_out[i] = columns[:, i * HEAD_DIM : (i + 1) * HEAD_DIM]

    @pl.when(jnp.logical_not(is_value))
    def _():
        for i in range(per_dev):
            head = columns[:, i * HEAD_DIM : (i + 1) * HEAD_DIM].astype(jnp.float32)
            heads_out[i] = rotate(head, cos_tab[...], sin_tab[...]).astype(jnp.bfloat16)

    fan = (GROUP - 2) // per_dev + 2

    def send_heads(first_dev, buf, kind, act):
        for i in range(per_dev):
            head = (me - first_dev) * per_dev + i
            for j in range(fan):
                target = (head * GROUP) // per_dev + j

                @pl.when(target <= (head * GROUP + GROUP - 1) // per_dev)
                def _():
                    slot = head - (target * per_dev) // GROUP
                    act(pltpu.make_async_remote_copy(
                        src_ref=heads_out.at[i], dst_ref=buf.at[slot],
                        send_sem=kv_send.at[i, j], recv_sem=kv_recv.at[kind, slot],
                        device_id={"tensor": target}, device_id_type=MESH,
                    ))

    @pl.when(is_key)
    def _():
        send_heads(q_devs, k_buf, 0, lambda copy: copy.start())

    @pl.when(is_value)
    def _():
        send_heads(q_devs + kv_devs, v_buf, 1, lambda copy: copy.start())

    @pl.when(is_query)
    def _():
        first = (me * per_dev) // GROUP
        last = (me * per_dev + per_dev - 1) // GROUP

        def kv_arrived(slot):
            for kind, buf in ((0, k_buf), (1, v_buf)):
                pltpu.make_async_remote_copy(
                    src_ref=buf.at[slot], dst_ref=buf.at[slot], send_sem=kv_send.at[0, 0],
                    recv_sem=kv_recv.at[kind, slot], device_id={"tensor": peer(1)}, device_id_type=MESH,
                ).wait_recv()

        kv_arrived(0)

        @pl.when(last > first)
        def _():
            kv_arrived(1)

        q_pos = lax.broadcasted_iota(jnp.int32, (size, size), 0)
        k_pos = lax.broadcasted_iota(jnp.int32, (size, size), 1)
        allowed = k_pos <= q_pos
        for i in range(per_dev):
            slot = (me * per_dev + i) // GROUP - first
            scores = lax.dot_general(
                heads_out[i], k_buf[slot], (((1,), (1,)), ((), ())),
                preferred_element_type=jnp.float32,
            ) * np.float32(1.0 / np.sqrt(HEAD_DIM))
            scores = jnp.where(allowed, scores, -1e30)
            top = jnp.max(scores, axis=1, keepdims=True)
            weights = jnp.where(allowed, jnp.exp(scores - top), 0.0)
            summed = jnp.dot(
                weights.astype(jnp.bfloat16), v_buf[slot], preferred_element_type=jnp.float32
            )
            mixed = summed / jnp.sum(weights, axis=1, keepdims=True)
            mix_all[me, :, i * HEAD_DIM : (i + 1) * HEAD_DIM] = mixed.astype(jnp.bfloat16)

        @pl.loop(1, n)
        def _(distance):
            remote(1, mix_all.at[me], mix_all.at[me], peer(distance)).start()

    @pl.loop(0, q_devs)
    def _(source):
        @pl.when(source != me)
        def _():
            arrived(1, source, mix_all.at[source])

    weight[1].wait()
    depth = w_qkv.shape[1]

    def out_project(source, total):
        here = pl.ds(pl.multiple_of(source * depth, depth), depth)
        return total + jnp.dot(
            mix_all[source], w_out[here, :], preferred_element_type=jnp.float32
        )

    att_own[...] = lax.fori_loop(
        0, q_devs, out_project, jnp.zeros((size, out_cols), jnp.float32)
    ).astype(jnp.bfloat16)
    att_all[me] = att_own[...]

    @pl.loop(1, n)
    def _(distance):
        remote(2, att_own, att_all.at[me], peer(distance)).start()

    @pl.loop(1, n)
    def _(distance):
        source = lax.rem(me + n - distance, n)
        arrived(2, source, att_all.at[source])

    per_att = CHUNK // out_cols

    def add_residual(chunk, total):
        attended = jnp.concatenate(
            [att_all[chunk * per_att + i].astype(jnp.float32) for i in range(per_att)], axis=1
        )
        for i in range(per_chunk):
            here = pl.ds(chunk * per_chunk + i, size, stride=tiles)
            value = tok_f32[here, :] + attended[:, i * LANES : (i + 1) * LANES]
            tok_f32[here, :] = value
            res_all[chunk, :, i * LANES : (i + 1) * LANES] = value
            total = total + value * value
        return total

    total = lax.fori_loop(0, chunks, add_residual, jnp.zeros((size, LANES), jnp.float32))
    scale2 = lax.rsqrt(jnp.sum(total, axis=1, keepdims=True) / width + 1e-05)
    weight[2].wait()
    weight[3].wait()

    def gate_up(chunk, totals):
        pieces = []
        for i in range(per_chunk):
            gain = moe_gain[pl.ds(chunk * per_chunk + i, 1), :]
            value = res_all[chunk, :, i * LANES : (i + 1) * LANES]
            pieces.append((value * scale2 * gain).astype(jnp.bfloat16))
        x = jnp.concatenate(pieces, axis=1)
        here = pl.ds(pl.multiple_of(chunk * CHUNK, CHUNK), CHUNK)
        return (
            totals[0] + jnp.dot(x, w_gate[here, :], preferred_element_type=jnp.float32),
            totals[1] + jnp.dot(x, w_up[here, :], preferred_element_type=jnp.float32),
        )

    zeros = jnp.zeros((size, w_gate.shape[1]), jnp.float32)
    gate, up = lax.fori_loop(0, chunks, gate_up, (zeros, zeros))
    hidden = (gate * (1.0 / (1.0 + jnp.exp(-gate))) * up).astype(jnp.bfloat16)
    weight[4].wait()

    @pl.loop(0, chunks)
    def _(chunk):
        here = pl.ds(pl.multiple_of(chunk * CHUNK, CHUNK), CHUNK)
        part = jnp.dot(hidden, w_down[:, here], preferred_element_type=jnp.float32)
        for i in range(per_chunk):
            part_f32[pl.ds(chunk * per_chunk + i, size, stride=tiles), :] = part[
                :, i * LANES : (i + 1) * LANES
            ]

    part_all[...] = part_f32[...].astype(jnp.bfloat16)

    @pl.loop(1, n)
    def _(distance):
        target = peer(distance)
        remote(3, token_block(part_all, target), part_in.at[me], target).start()

    part_in[me] = part_all[my_block, :]

    @pl.loop(1, n)
    def _(distance):
        source = lax.rem(me + n - distance, n)
        arrived(3, source, part_in.at[source])

    owners = n // EXPERT_WINDOW
    picked = [
        [
            sum(jnp.where(ids[row, k] == e, gates[row, k], 0.0) for k in range(2))
            for e in range(EXPERT_WINDOW)
        ]
        for row in range(rows)
    ]
    residual = tok_f32[my_block, :]
    for row in range(rows):
        total = residual[row * tiles : (row + 1) * tiles, :]
        for e in range(EXPERT_WINDOW):
            expert = lax.fori_loop(
                0, owners,
                lambda j, acc: acc + part_in[
                    e * owners + j, row * tiles : (row + 1) * tiles, :
                ].astype(jnp.float32),
                jnp.zeros((tiles, LANES), jnp.float32),
            )
            total = total + picked[row][e] * expert
        out[row * tiles : (row + 1) * tiles, :] = total.astype(jnp.bfloat16)

    @pl.when(is_key)
    def _():
        send_heads(q_devs, k_buf, 0, lambda copy: copy.wait_send())

    @pl.when(is_value)
    def _():
        send_heads(q_devs + kv_devs, v_buf, 1, lambda copy: copy.wait_send())

    @pl.loop(1, n)
    def _(distance):
        target = peer(distance)
        remote(0, token_block(tok_all, me), token_block(tok_all, me), target).wait_send()
        remote(2, att_own, att_all.at[me], target).wait_send()
        remote(3, token_block(part_all, target), part_in.at[me], target).wait_send()

        @pl.when(is_query)
        def _():
            remote(1, mix_all.at[me], mix_all.at[me], target).wait_send()


def on_device(
    tokens, attn_gain, w_qkv, w_out, moe_gain, w_gate, w_up, w_down, expert_ids, gate_weights
):
    n = lax.axis_size("tensor")
    rows, width = tokens.shape
    size = rows * n
    tiles = width // LANES
    block = rows * tiles
    per_dev = w_qkv.shape[1] // HEAD_DIM
    q_devs = HEADS // per_dev
    fan = (GROUP - 2) // per_dev + 2
    cosine, sine = rotation_tables(size)
    bf16, f32 = jnp.bfloat16, jnp.float32
    any_space = pl.BlockSpec(memory_space=pl.ANY)
    scalar_space = pl.BlockSpec(memory_space=pltpu.SMEM)
    result = pl.pallas_call(
        functools.partial(kernel, n),
        out_shape=jax.ShapeDtypeStruct((block, LANES), bf16),
        in_specs=[any_space] * 10 + [scalar_space] * 2,
        out_specs=pl.BlockSpec(memory_space=pltpu.VMEM),
        scratch_shapes=[
            pltpu.VMEM(w_qkv.shape, bf16),
            pltpu.VMEM(w_out.shape, bf16),
            pltpu.VMEM(w_gate.shape, bf16),
            pltpu.VMEM(w_up.shape, bf16),
            pltpu.VMEM(w_down.shape, bf16),
            pltpu.VMEM(tokens.shape, bf16),
            pltpu.VMEM((tiles, LANES), f32),
            pltpu.VMEM((tiles, LANES), f32),
            pltpu.VMEM((size, HEAD_DIM), f32),
            pltpu.VMEM((size, HEAD_DIM), f32),
            pltpu.VMEM((block, LANES), f32),
            pltpu.VMEM((n * block, LANES), bf16),
            pltpu.VMEM((n * block, LANES), f32),
            pltpu.VMEM((width // CHUNK, size, CHUNK), bf16),
            pltpu.VMEM((size, w_qkv.shape[1]), bf16),
            pltpu.VMEM((per_dev, size, HEAD_DIM), bf16),
            pltpu.VMEM((2, size, HEAD_DIM), bf16),
            pltpu.VMEM((2, size, HEAD_DIM), bf16),
            pltpu.VMEM((q_devs, size, w_qkv.shape[1]), bf16),
            pltpu.VMEM((size, w_out.shape[1]), bf16),
            pltpu.VMEM((n, size, w_out.shape[1]), bf16),
            pltpu.VMEM((width // CHUNK, size, CHUNK), f32),
            pltpu.VMEM((n * block, LANES), f32),
            pltpu.VMEM((n * block, LANES), bf16),
            pltpu.VMEM((n, block, LANES), bf16),
            pltpu.SemaphoreType.DMA((5,)),
            pltpu.SemaphoreType.DMA((5,)),
            pltpu.SemaphoreType.DMA((4, n)),
            pltpu.SemaphoreType.DMA((4, n)),
            pltpu.SemaphoreType.DMA((per_dev, fan)),
            pltpu.SemaphoreType.DMA((2, 2)),
        ],
        compiler_params=pltpu.CompilerParams(
            collective_id=0, has_side_effects=True, vmem_limit_bytes=56 * 1024 * 1024
        ),
        name="layer",
    )(
        tokens, attn_gain.reshape(tiles, LANES), w_qkv, w_out, moe_gain.reshape(tiles, LANES),
        w_gate, w_up, w_down, jnp.asarray(cosine), jnp.asarray(sine), expert_ids, gate_weights,
    )
    return result.reshape(rows, width)


def solution(mesh):
    return jax.shard_map(
        on_device,
        mesh=mesh,
        in_specs=(
            P(("groups", "tensor"), None),
            P(),
            P(None, "tensor"),
            P(None, "tensor"),
            P(),
            P(None, "tensor"),
            P(None, "tensor"),
            P("tensor", None),
            P(("groups", "tensor"), None),
            P(("groups", "tensor"), None),
        ),
        out_specs=P(("groups", "tensor"), None),
        check_vma=False,
    )
```

time: 285 us -> 68.4 us (0.24)
  the two profiles are of different devices: /device:TPU:0 before, /device:TPU:25 now
where the time goes in v1:
time: 68.4 us; the launch traced here: 68.2 us
  Pallas kernels  66.8 us (98%)
  local copies, waits for them, and re-layouts  1.36 us (2%)
    pallas_call x1, Pallas kernels, on_device(): pl.pallas_call(functools.partial(kernel, n), out_shape=jax.ShapeDtypeStru...  66.8 us

profile of v1, /device:TPU:25, one launch (start us, length us, event | category | flops | bytes accessed | tf_op | source)
XLA Modules:
  0.0 68.2 jit_solution(1800567908140228699)
XLA Ops:
  0.0 66.8 %layer.1 = bf16[96,128]{1,0:T(8,128)(2,1)} custom-call(bf16[2,6144]{1,0:T(2,128)(2,1)} %tok_in.1, f32[48,128]{1,0:T(8,128)} %bitcast.2, bf16[6144,512]{1,0:T(8,128)(2,1)} %w_qkv_in.1, bf16[6144,384]{1,0:T(8,128)(2,1)} %w_out_in.1, f32[48,128]{1,0:T(8,128)} %bitcast.3, bf16[6144,256]{1,0:T(8,128)(2,1)} %w_gate_in.1, bf16[6144,256]{1,0:T(8,128)(2,1)} %w_up_in.1, ...), custom_call_target="tpu_custom_call" | custom-call | tf_op jit(solution)/shard_map/layer/pallas_call | solution.py:379
  66.8 1.4 %reshape.11 = bf16[2,6144]{1,0:T(2,128)(2,1)} reshape(bf16[96,128]{1,0:T(8,128)(2,1)} %layer.1) | data formatting | bytes 49152 | tf_op jit(solution)/shard_map/reshape | solution.py:425

commit v2 on v1

v2 whole, which is shorter than its diff:
```python
import functools

import jax
import jax.numpy as jnp
import numpy as np
from jax import lax
from jax.experimental import pallas as pl
from jax.experimental.pallas import tpu as pltpu
from jax.sharding import PartitionSpec as P

HEADS = 48
KV_HEADS = 8
GROUP = HEADS // KV_HEADS
HEAD_DIM = 128
EXPERT_WINDOW = 2
LANES = 128
CHUNK = 768
MESH = pl.DeviceIdType.MESH


def rotation_tables(size):
    half = HEAD_DIM // 2
    inverse = np.float32(1000000.0) ** (-(np.arange(half, dtype=np.float32) * 2.0) / HEAD_DIM)
    angles = np.arange(size, dtype=np.float32)[:, None] * inverse.astype(np.float32)[None, :]
    cosine, sine = np.cos(angles), np.sin(angles)
    return (
        np.concatenate([cosine, cosine], axis=1).astype(np.float32),
        np.concatenate([-sine, sine], axis=1).astype(np.float32),
    )


def rotate(head, cosine, sine):
    half = HEAD_DIM // 2
    swapped = jnp.concatenate([head[:, half:], head[:, :half]], axis=1)
    return head * cosine + swapped * sine


def kernel(
    n, tok_in, attn_gain_in, w_qkv_in, w_out_in, moe_gain_in, w_gate_in, w_up_in, w_down_in,
    cos_in, sin_in, ids, gates, out,
    w_qkv, w_out, w_gate, w_up, w_down, own_tok, attn_gain, moe_gain, cos_tab, sin_tab,
    stage, tok_all, tok_f32, heads, att_all, gate_sum, up_sum, square_sum,
    part_f32, part_all, pair_in, pair_out, part_in,
    small_sem, weight_sem, send_sem, relay_sem, recv_sem, pair_sem,
):
    me = lax.axis_index("tensor")
    core = lax.rem(me, 2)
    chip = me // 2
    partner = me + 1 - 2 * core
    chips = n // 2
    size = gate_sum.shape[0]
    tiles = attn_gain.shape[0]
    width = tiles * LANES
    rows = stage.shape[0] // tiles
    block = rows * tiles
    per_dev = w_qkv.shape[1] // HEAD_DIM
    chunks = width // CHUNK
    per_chunk = CHUNK // LANES
    out_cols = w_out.shape[1]

    small = [
        pltpu.make_async_copy(src, dst, small_sem.at[i])
        for i, (src, dst) in enumerate(
            [(tok_in, own_tok), (attn_gain_in, attn_gain), (moe_gain_in, moe_gain),
             (cos_in, cos_tab), (sin_in, sin_tab)]
        )
    ]
    weight = [
        pltpu.make_async_copy(src, dst, weight_sem.at[i])
        for i, (src, dst) in enumerate(
            [(w_qkv_in, w_qkv), (w_out_in, w_out), (w_gate_in, w_gate), (w_up_in, w_up),
             (w_down_in, w_down)]
        )
    ]
    for copy in small:
        copy.start()
    for copy in weight:
        copy.start()

    def chip_at(step):
        z = lax.rem(chip // 2 + step // 2, chips // 2)
        return z * 2 + lax.rem(chip + step, 2)

    def chip_from(step):
        z = lax.rem(chip // 2 + chips // 2 - step // 2, chips // 2)
        return z * 2 + lax.rem(chip + step, 2)

    barrier = pltpu.get_barrier_semaphore()
    pl.semaphore_signal(barrier, inc=1, device_id={"tensor": partner}, device_id_type=MESH)

    @pl.loop(1, chips)
    def _(step):
        pl.semaphore_signal(
            barrier, inc=1, device_id={"tensor": chip_at(step) * 2 + core}, device_id_type=MESH
        )

    small[0].wait()
    for tile in range(tiles):
        piece = own_tok[:, tile * LANES : (tile + 1) * LANES].astype(jnp.float32)
        for row in range(rows):
            stage[row * tiles + tile : row * tiles + tile + 1, :] = piece[row : row + 1, :]
    tok_all[me] = stage[...].astype(jnp.bfloat16)
    my_block = pl.ds(pl.multiple_of(me * block, 16), block)
    tok_f32[my_block, :] = stage[...]
    pl.semaphore_wait(barrier, chips)

    def transfer(phase, src, dst, target, send, slot):
        return pltpu.make_async_remote_copy(
            src_ref=src, dst_ref=dst, send_sem=send, recv_sem=recv_sem.at[phase, slot],
            device_id={"tensor": target}, device_id_type=MESH,
        )

    def direct(phase, ref, step):
        return transfer(
            phase, ref.at[me], ref.at[me], chip_at(step) * 2 + core, send_sem.at[phase, step], me
        )

    def relay(phase, ref, step):
        source = chip_from(step) * 2 + core
        return transfer(
            phase, ref.at[source], ref.at[source], partner, relay_sem.at[phase, step], source
        )

    def arrived(phase, ref, source):
        transfer(
            phase, ref.at[source], ref.at[source], partner, relay_sem.at[phase, 0], source
        ).wait_recv()

    def gather(phase, ref, consume):
        @pl.loop(1, chips)
        def _(step):
            direct(phase, ref, chips - step).start()

        relay(phase, ref, 0).start()
        if consume is not None:
            consume(me)

        def take_direct(step):
            source = chip_from(step) * 2 + core
            arrived(phase, ref, source)
            relay(phase, ref, step).start()
            if consume is not None:
                consume(source)

        def take_relayed(step):
            source = chip_from(step) * 2 + 1 - core
            arrived(phase, ref, source)
            if consume is not None:
                consume(source)

        lag = min(4, chips)
        pl.loop(1, lag)(take_direct)

        @pl.loop(lag, chips)
        def _(step):
            take_direct(step)
            take_relayed(step - lag)

        pl.loop(chips - lag, chips)(take_relayed)

    def gather_left(phase, ref):
        @pl.loop(0, chips)
        def _(step):
            relay(phase, ref, step).wait_send()

        @pl.loop(1, chips)
        def _(step):
            direct(phase, ref, step).wait_send()

    def widen(source):
        here = pl.ds(pl.multiple_of(source * block, 16), block)
        tok_f32[here, :] = tok_all[source].astype(jnp.float32)

    gather(0, tok_all, widen)
    for copy in small[1:]:
        copy.wait()

    def tok_tile(tile):
        return tok_f32[pl.ds(tile, size, stride=tiles), :]

    def add_squares(chunk, total):
        for i in range(per_chunk):
            value = tok_tile(chunk * per_chunk + i)
            total = total + value * value
        return total

    total = lax.fori_loop(0, chunks, add_squares, jnp.zeros((size, LANES), jnp.float32))
    scale = lax.rsqrt(jnp.sum(total, axis=1, keepdims=True) / width + 1e-05)
    weight[0].wait()

    def project(chunk, total):
        pieces = []
        for i in range(per_chunk):
            tile = chunk * per_chunk + i
            pieces.append((tok_tile(tile) * scale * attn_gain[pl.ds(tile, 1), :]).astype(jnp.bfloat16))
        here = pl.ds(pl.multiple_of(chunk * CHUNK, CHUNK), CHUNK)
        return total + jnp.dot(
            jnp.concatenate(pieces, axis=1), w_qkv[here, :], preferred_element_type=jnp.float32
        )

    columns = lax.fori_loop(
        0, chunks, project, jnp.zeros((size, w_qkv.shape[1]), jnp.float32)
    ).astype(jnp.bfloat16)

    turns = jnp.where(me * per_dev >= HEADS + KV_HEADS, 0.0, 1.0)
    cosine = cos_tab[...] * turns + (1.0 - turns)
    sine = sin_tab[...] * turns
    for i in range(per_dev):
        head = columns[:, i * HEAD_DIM : (i + 1) * HEAD_DIM].astype(jnp.float32)
        heads[me, i] = rotate(head, cosine, sine).astype(jnp.bfloat16)

    gather(1, heads, None)
    weight[1].wait()

    q_pos = lax.rem(lax.broadcasted_iota(jnp.int32, (GROUP * size, size), 0), size)
    k_pos = lax.broadcasted_iota(jnp.int32, (GROUP * size, size), 1)
    allowed = k_pos <= q_pos

    def head_at(index):
        return heads[index // per_dev, lax.rem(index, per_dev)]

    def attend(g, total):
        queries = jnp.concatenate([head_at(g * GROUP + i) for i in range(GROUP)], axis=0)
        scores = lax.dot_general(
            queries, head_at(HEADS + g), (((1,), (1,)), ((), ())),
            preferred_element_type=jnp.float32,
        ) * np.float32(1.0 / np.sqrt(HEAD_DIM))
        scores = jnp.where(allowed, scores, -1e30)
        top = jnp.max(scores, axis=1, keepdims=True)
        weights = jnp.where(allowed, jnp.exp(scores - top), 0.0)
        summed = jnp.dot(
            weights.astype(jnp.bfloat16), head_at(HEADS + KV_HEADS + g),
            preferred_element_type=jnp.float32,
        )
        mixed = (summed / jnp.sum(weights, axis=1, keepdims=True)).astype(jnp.bfloat16)
        mixed = jnp.concatenate([mixed[i * size : (i + 1) * size] for i in range(GROUP)], axis=1)
        depth = GROUP * HEAD_DIM
        here = pl.ds(pl.multiple_of(g * depth, depth), depth)
        return total + jnp.dot(mixed, w_out[here, :], preferred_element_type=jnp.float32)

    att_all[me] = lax.fori_loop(
        0, KV_HEADS, attend, jnp.zeros((size, out_cols), jnp.float32)
    ).astype(jnp.bfloat16)

    gate_sum[...] = jnp.zeros_like(gate_sum)
    up_sum[...] = jnp.zeros_like(up_sum)
    square_sum[...] = jnp.zeros_like(square_sum)
    weight[2].wait()
    weight[3].wait()

    def expert_input(index, attended):
        wide = attended.shape[1]
        pieces = []
        total = square_sum[...]
        for i in range(wide // LANES):
            tile = index * (wide // LANES) + i
            here = pl.ds(tile, size, stride=tiles)
            value = tok_f32[here, :] + attended[:, i * LANES : (i + 1) * LANES]
            tok_f32[here, :] = value
            total = total + value * value
            pieces.append((value * moe_gain[pl.ds(tile, 1), :]).astype(jnp.bfloat16))
        square_sum[...] = total
        x = jnp.concatenate(pieces, axis=1)
        here = pl.ds(pl.multiple_of(index * wide, LANES), wide)
        gate_sum[...] += jnp.dot(x, w_gate[here, :], preferred_element_type=jnp.float32)
        up_sum[...] += jnp.dot(x, w_up[here, :], preferred_element_type=jnp.float32)

    if out_cols % LANES == 0:
        gather(2, att_all, lambda source: expert_input(source, att_all[source].astype(jnp.float32)))
    else:
        gather(2, att_all, None)
        joined = CHUNK // out_cols

        @pl.loop(0, chunks)
        def _(chunk):
            expert_input(chunk, jnp.concatenate(
                [att_all[chunk * joined + i].astype(jnp.float32) for i in range(joined)], axis=1
            ))

    scale = lax.rsqrt(jnp.sum(square_sum[...], axis=1, keepdims=True) / width + 1e-05)
    gate = gate_sum[...] * scale
    hidden = (gate * (1.0 / (1.0 + jnp.exp(-gate))) * (up_sum[...] * scale)).astype(jnp.bfloat16)
    weight[4].wait()

    @pl.loop(0, chunks)
    def _(chunk):
        here = pl.ds(pl.multiple_of(chunk * CHUNK, CHUNK), CHUNK)
        part = jnp.dot(hidden, w_down[:, here], preferred_element_type=jnp.float32)
        for i in range(per_chunk):
            part_f32[pl.ds(chunk * per_chunk + i, size, stride=tiles), :] = part[
                :, i * LANES : (i + 1) * LANES
            ]

    @pl.loop(0, n)
    def _(index):
        here = pl.ds(pl.multiple_of(index * block, 16), block)
        part_all[lax.rem(index, 2), index // 2] = part_f32[here, :].astype(jnp.bfloat16)

    pair = pltpu.make_async_remote_copy(
        src_ref=part_all.at[1 - core], dst_ref=pair_in, send_sem=pair_sem.at[0],
        recv_sem=pair_sem.at[1], device_id={"tensor": partner}, device_id_type=MESH,
    )
    pair.start()
    pair.wait_recv()

    def summed(index):
        return part_all[core, index].astype(jnp.float32) + pair_in[index].astype(jnp.float32)

    def deliver(step):
        target = chip_at(step)
        return transfer(
            3, pair_out.at[target], part_in.at[chip], target * 2 + core, send_sem.at[3, step], chip
        )

    @pl.loop(1, chips)
    def _(step):
        target = chip_at(chips - step)
        pair_out[target] = summed(target).astype(jnp.bfloat16)
        deliver(chips - step).start()

    part_in[chip] = summed(chip).astype(jnp.bfloat16)

    picked = [
        [
            sum(jnp.where(ids[row, k] == e, gates[row, k], 0.0) for k in range(2))
            for e in range(EXPERT_WINDOW)
        ]
        for row in range(rows)
    ]
    gather_left(0, tok_all)
    gather_left(1, heads)
    gather_left(2, att_all)
    pair.wait_send()

    @pl.loop(1, chips)
    def _(step):
        source = chip_from(step)
        transfer(
            3, part_in.at[source], part_in.at[source], partner, send_sem.at[3, 0], source
        ).wait_recv()

    owners = chips // EXPERT_WINDOW
    residual = tok_f32[my_block, :]
    for row in range(rows):
        total = residual[row * tiles : (row + 1) * tiles, :]
        for e in range(EXPERT_WINDOW):
            expert = jnp.zeros((tiles, LANES), jnp.float32)
            for j in range(owners):
                expert = expert + part_in[
                    e * owners + j, row * tiles : (row + 1) * tiles, :
                ].astype(jnp.float32)
            total = total + picked[row][e] * expert
        out[row * tiles : (row + 1) * tiles, :] = total.astype(jnp.bfloat16)

    @pl.loop(1, chips)
    def _(step):
        deliver(step).wait_send()


def on_device(
    tokens, attn_gain, w_qkv, w_out, moe_gain, w_gate, w_up, w_down, expert_ids, gate_weights
):
    n = lax.axis_size("tensor")
    rows, width = tokens.shape
    size = rows * n
    tiles = width // LANES
    block = rows * tiles
    per_dev = w_qkv.shape[1] // HEAD_DIM
    cosine, sine = rotation_tables(size)
    bf16, f32 = jnp.bfloat16, jnp.float32
    any_space = pl.BlockSpec(memory_space=pl.ANY)
    scalar_space = pl.BlockSpec(memory_space=pltpu.SMEM)
    result = pl.pallas_call(
        functools.partial(kernel, n),
        out_shape=jax.ShapeDtypeStruct((block, LANES), bf16),
        in_specs=[any_space] * 10 + [scalar_space] * 2,
        out_specs=pl.BlockSpec(memory_space=pltpu.VMEM),
        scratch_shapes=[
            pltpu.VMEM(w_qkv.shape, bf16),
            pltpu.VMEM(w_out.shape, bf16),
            pltpu.VMEM(w_gate.shape, bf16),
            pltpu.VMEM(w_up.shape, bf16),
            pltpu.VMEM(w_down.shape, bf16),
            pltpu.VMEM(tokens.shape, bf16),
            pltpu.VMEM((tiles, LANES), f32),
            pltpu.VMEM((tiles, LANES), f32),
            pltpu.VMEM((size, HEAD_DIM), f32),
            pltpu.VMEM((size, HEAD_DIM), f32),
            pltpu.VMEM((block, LANES), f32),
            pltpu.VMEM((n, block, LANES), bf16),
            pltpu.VMEM((n * block, LANES), f32),
            pltpu.VMEM((n, per_dev, size, HEAD_DIM), bf16),
            pltpu.VMEM((n, size, w_out.shape[1]), bf16),
            pltpu.VMEM((size, w_gate.shape[1]), f32),
            pltpu.VMEM((size, w_up.shape[1]), f32),
            pltpu.VMEM((size, LANES), f32),
            pltpu.VMEM((n * block, LANES), f32),
            pltpu.VMEM((2, n // 2, block, LANES), bf16),
            pltpu.VMEM((n // 2, block, LANES), bf16),
            pltpu.VMEM((n // 2, block, LANES), bf16),
            pltpu.VMEM((n // 2, block, LANES), bf16),
            pltpu.SemaphoreType.DMA((5,)),
            pltpu.SemaphoreType.DMA((5,)),
            pltpu.SemaphoreType.DMA((4, n // 2)),
            pltpu.SemaphoreType.DMA((3, n // 2)),
            pltpu.SemaphoreType.DMA((4, n)),
            pltpu.SemaphoreType.DMA((2,)),
        ],
        compiler_params=pltpu.CompilerParams(
            collective_id=0, has_side_effects=True, vmem_limit_bytes=56 * 1024 * 1024
        ),
        name="layer",
    )(
        tokens, attn_gain.reshape(tiles, LANES), w_qkv, w_out, moe_gain.reshape(tiles, LANES),
        w_gate, w_up, w_down, jnp.asarray(cosine), jnp.asarray(sine), expert_ids, gate_weights,
    )
    return result.reshape(rows, width)


def solution(mesh):
    return jax.shard_map(
        on_device,
        mesh=mesh,
        in_specs=(
            P(("groups", "tensor"), None),
            P(),
            P(None, "tensor"),
            P(None, "tensor"),
            P(),
            P(None, "tensor"),
            P(None, "tensor"),
            P("tensor", None),
            P(("groups", "tensor"), None),
            P(("groups", "tensor"), None),
        ),
        out_specs=P(("groups", "tensor"), None),
        check_vma=False,
    )
```

time: 68.4 us -> 49.9 us (0.73)
  the two profiles are of different devices: /device:TPU:25 before, /device:TPU:0 now
where the time goes in v2:
time: 49.9 us; the launch traced here: 49.7 us
  Pallas kernels  48.4 us (97%)
  local copies, waits for them, and re-layouts  1.36 us (3%)
    pallas_call x1, Pallas kernels, on_device(): pl.pallas_call(functools.partial(kernel, n), out_shape=jax.ShapeDtypeStru...  48.4 us
    reshape x1, local copies, waits for them, and re-layouts, on_device(): return result.reshape(rows, width)  1.36 us

profile of v2, /device:TPU:0, one launch (start us, length us, event | category | flops | bytes accessed | tf_op | source)
XLA Modules:
  0.0 49.7 jit_solution(3487250504525490089)
XLA Ops:
  0.0 48.4 %layer.1 = bf16[96,128]{1,0:T(8,128)(2,1)} custom-call(bf16[2,6144]{1,0:T(2,128)(2,1)} %tok_in.1, f32[48,128]{1,0:T(8,128)} %bitcast.2, bf16[6144,512]{1,0:T(8,128)(2,1)} %w_qkv_in.1, bf16[6144,384]{1,0:T(8,128)(2,1)} %w_out_in.1, f32[48,128]{1,0:T(8,128)} %bitcast.3, bf16[6144,256]{1,0:T(8,128)(2,1)} %w_gate_in.1, bf16[6144,256]{1,0:T(8,128)(2,1)} %w_up_in.1, ...), custom_call_target="tpu_custom_call" | custom-call | tf_op jit(solution)/shard_map/layer/pallas_call | solution.py:373
  48.4 1.4 %reshape.11 = bf16[2,6144]{1,0:T(2,128)(2,1)} reshape(bf16[96,128]{1,0:T(8,128)(2,1)} %layer.1) | data formatting | bytes 49152 | tf_op jit(solution)/shard_map/reshape | solution.py:417

commit v3 on v2

--- a/solution.py
+++ b/solution.py
@@ -37,9 +37,9 @@
 
 def kernel(
     n, tok_in, attn_gain_in, w_qkv_in, w_out_in, moe_gain_in, w_gate_in, w_up_in, w_down_in,
-    cos_in, sin_in, ids, gates, out,
+    cos_in, sin_in, ids_in, gates_in, out,
     w_qkv, w_out, w_gate, w_up, w_down, own_tok, attn_gain, moe_gain, cos_tab, sin_tab,
-    stage, tok_all, tok_f32, heads, att_all, gate_sum, up_sum, square_sum,
+    ids, gates, stage, tok_all, tok_f32, heads, att_all, gate_sum, up_sum, square_sum,
     part_f32, part_all, pair_in, pair_out, part_in,
     small_sem, weight_sem, send_sem, relay_sem, recv_sem, pair_sem,
 ):
@@ -62,7 +62,7 @@
         pltpu.make_async_copy(src, dst, small_sem.at[i])
         for i, (src, dst) in enumerate(
             [(tok_in, own_tok), (attn_gain_in, attn_gain), (moe_gain_in, moe_gain),
-             (cos_in, cos_tab), (sin_in, sin_tab)]
+             (cos_in, cos_tab), (sin_in, sin_tab), (ids_in, ids), (gates_in, gates)]
         )
     ]
     weight = [
@@ -178,29 +178,26 @@
     def tok_tile(tile):
         return tok_f32[pl.ds(tile, size, stride=tiles), :]
 
-    def add_squares(chunk, total):
-        for i in range(per_chunk):
-            value = tok_tile(chunk * per_chunk + i)
-            total = total + value * value
-        return total
-
-    total = lax.fori_loop(0, chunks, add_squares, jnp.zeros((size, LANES), jnp.float32))
-    scale = lax.rsqrt(jnp.sum(total, axis=1, keepdims=True) / width + 1e-05)
     weight[0].wait()
 
-    def project(chunk, total):
+    def project(chunk, totals):
+        product, squares = totals
         pieces = []
         for i in range(per_chunk):
             tile = chunk * per_chunk + i
-            pieces.append((tok_tile(tile) * scale * attn_gain[pl.ds(tile, 1), :]).astype(jnp.bfloat16))
+            value = tok_tile(tile)
+            squares = squares + value * value
+            pieces.append((value * attn_gain[pl.ds(tile, 1), :]).astype(jnp.bfloat16))
         here = pl.ds(pl.multiple_of(chunk * CHUNK, CHUNK), CHUNK)
-        return total + jnp.dot(
-            jnp.concatenate(pieces, axis=1), w_qkv[here, :], preferred_element_type=jnp.float32
-        )
-
-    columns = lax.fori_loop(
-        0, chunks, project, jnp.zeros((size, w_qkv.shape[1]), jnp.float32)
-    ).astype(jnp.bfloat16)
+        x = jnp.concatenate(pieces, axis=1)
+        return product + jnp.dot(x, w_qkv[here, :], preferred_element_type=jnp.float32), squares
+
+    product, squares = lax.fori_loop(
+        0, chunks, project,
+        (jnp.zeros((size, w_qkv.shape[1]), jnp.float32), jnp.zeros((size, LANES), jnp.float32)),
+    )
+    scale = lax.rsqrt(jnp.sum(squares, axis=1, keepdims=True) / width + 1e-05)
+    columns = (product * scale).astype(jnp.bfloat16)
 
     turns = jnp.where(me * per_dev >= HEADS + KV_HEADS, 0.0, 1.0)
     cosine = cos_tab[...] * turns + (1.0 - turns)
@@ -239,7 +236,7 @@
         return total + jnp.dot(mixed, w_out[here, :], preferred_element_type=jnp.float32)
 
     att_all[me] = lax.fori_loop(
-        0, KV_HEADS, attend, jnp.zeros((size, out_cols), jnp.float32)
+        0, KV_HEADS, attend, jnp.zeros((size, out_cols), jnp.float32), unroll=8
     ).astype(jnp.bfloat16)
 
     gate_sum[...] = jnp.zeros_like(gate_sum)
@@ -350,7 +347,11 @@
                     e * owners + j, row * tiles : (row + 1) * tiles, :
                 ].astype(jnp.float32)
             total = total + picked[row][e] * expert
-        out[row * tiles : (row + 1) * tiles, :] = total.astype(jnp.bfloat16)
+        stage[row * tiles : (row + 1) * tiles, :] = total
+    for tile in range(tiles):
+        out[:, tile * LANES : (tile + 1) * LANES] = stage[
+            pl.ds(tile, rows, stride=tiles), :
+        ].astype(jnp.bfloat16)
 
     @pl.loop(1, chips)
     def _(step):
@@ -369,11 +370,10 @@
     cosine, sine = rotation_tables(size)
     bf16, f32 = jnp.bfloat16, jnp.float32
     any_space = pl.BlockSpec(memory_space=pl.ANY)
-    scalar_space = pl.BlockSpec(memory_space=pltpu.SMEM)
     result = pl.pallas_call(
         functools.partial(kernel, n),
-        out_shape=jax.ShapeDtypeStruct((block, LANES), bf16),
-        in_specs=[any_space] * 10 + [scalar_space] * 2,
+        out_shape=jax.ShapeDtypeStruct((rows, width), bf16),
+        in_specs=[any_space] * 12,
         out_specs=pl.BlockSpec(memory_space=pltpu.VMEM),
         scratch_shapes=[
             pltpu.VMEM(w_qkv.shape, bf16),
@@ -386,6 +386,8 @@
             pltpu.VMEM((tiles, LANES), f32),
             pltpu.VMEM((size, HEAD_DIM), f32),
             pltpu.VMEM((size, HEAD_DIM), f32),
+            pltpu.SMEM(expert_ids.shape, jnp.int32),
+            pltpu.SMEM(gate_weights.shape, f32),
             pltpu.VMEM((block, LANES), f32),
             pltpu.VMEM((n, block, LANES), bf16),
             pltpu.VMEM((n * block, LANES), f32),
@@ -399,7 +401,7 @@
             pltpu.VMEM((n // 2, block, LANES), bf16),
             pltpu.VMEM((n // 2, block, LANES), bf16),
             pltpu.VMEM((n // 2, block, LANES), bf16),
-            pltpu.SemaphoreType.DMA((5,)),
+            pltpu.SemaphoreType.DMA((7,)),
             pltpu.SemaphoreType.DMA((5,)),
             pltpu.SemaphoreType.DMA((4, n // 2)),
             pltpu.SemaphoreType.DMA((3, n // 2)),
@@ -414,7 +416,7 @@
         tokens, attn_gain.reshape(tiles, LANES), w_qkv, w_out, moe_gain.reshape(tiles, LANES),
         w_gate, w_up, w_down, jnp.asarray(cosine), jnp.asarray(sine), expert_ids, gate_weights,
     )
-    return result.reshape(rows, width)
+    return result
 
 
 def solution(mesh):

time: 49.9 us -> 47.9 us (0.960)
  Pallas kernels: 48.4 us -> 46.3 us
    pallas_call x1, Pallas kernels: 48.4 us -> 46.3 us  [on_device(): pl.pallas_call(functools.partial(kernel, n), out_shape=jax.ShapeDtypeStru...]
    unnamed x0 -> x1, local copies, waits for them, and re-layouts: none -> 1.36 us
    reshape x1 -> x0, local copies, waits for them, and re-layouts: 1.36 us -> none  [on_device(): return result.reshape(rows, width)]
where the time goes in v3:
time: 47.9 us; the launch traced here: 47.7 us
  Pallas kernels  46.3 us (97%)
  local copies, waits for them, and re-layouts  1.36 us (3%)
    pallas_call x1, Pallas kernels, on_device(): pl.pallas_call(functools.partial(kernel, n), out_shape=jax.ShapeDtypeStru...  46.3 us
    unnamed x1, local copies, waits for them, and re-layouts  1.36 us

profile of v3, /device:TPU:0, one launch (start us, length us, event | category | flops | bytes accessed | tf_op | source)
XLA Modules:
  0.0 47.7 jit_solution(14198262211153021320)
XLA Ops:
  0.0 46.3 %layer.1 = bf16[2,6144]{1,0:T(2,128)(2,1)} custom-call(bf16[2,6144]{1,0:T(2,128)(2,1)} %tok_in.1, f32[48,128]{1,0:T(8,128)} %bitcast.2, bf16[6144,512]{1,0:T(8,128)(2,1)} %w_qkv_in.1, bf16[6144,384]{1,0:T(8,128)(2,1)} %w_out_in.1, f32[48,128]{1,0:T(8,128)} %bitcast.3, bf16[6144,256]{1,0:T(8,128)(2,1)} %w_gate_in.1, bf16[6144,256]{1,0:T(8,128)(2,1)} %w_up_in.1, ...), custom_call_target="tpu_custom_call" | custom-call | tf_op jit(solution)/shard_map/layer/pallas_call | solution.py:373
  46.3 1.4 %copy.14 = bf16[2,6144]{1,0:T(2,128)(2,1)} copy(bf16[2,6144]{1,0:T(2,128)(2,1)} %layer.1) | data formatting | bytes 49152

commit v4 on v3

--- a/solution.py
+++ b/solution.py
@@ -15,6 +15,7 @@
 EXPERT_WINDOW = 2
 LANES = 128
 CHUNK = 768
+PIECE = 16
 MESH = pl.DeviceIdType.MESH
 
 
@@ -41,7 +42,7 @@
     w_qkv, w_out, w_gate, w_up, w_down, own_tok, attn_gain, moe_gain, cos_tab, sin_tab,
     ids, gates, stage, tok_all, tok_f32, heads, att_all, gate_sum, up_sum, square_sum,
     part_f32, part_all, pair_in, pair_out, part_in,
-    small_sem, weight_sem, send_sem, relay_sem, recv_sem, pair_sem,
+    small_sem, weight_sem, send_sem, relay_sem, recv_sem, pair_sem, out_send, out_recv,
 ):
     me = lax.axis_index("tensor")
     core = lax.rem(me, 2)
@@ -57,6 +58,8 @@
     chunks = width // CHUNK
     per_chunk = CHUNK // LANES
     out_cols = w_out.shape[1]
+    pieces = tiles // PIECE
+    share = rows * PIECE
 
     small = [
         pltpu.make_async_copy(src, dst, small_sem.at[i])
@@ -78,12 +81,10 @@
         copy.start()
 
     def chip_at(step):
-        z = lax.rem(chip // 2 + step // 2, chips // 2)
-        return z * 2 + lax.rem(chip + step, 2)
-
-    def chip_from(step):
-        z = lax.rem(chip // 2 + chips // 2 - step // 2, chips // 2)
-        return z * 2 + lax.rem(chip + step, 2)
+        bits = [2**b for b in range(chips.bit_length() - 1)]
+        return sum(lax.rem(chip // bit + step // bit, 2) * bit for bit in bits)
+
+    chip_from = chip_at
 
     barrier = pltpu.get_barrier_semaphore()
     pl.semaphore_signal(barrier, inc=1, device_id={"tensor": partner}, device_id_type=MESH)
@@ -279,43 +280,56 @@
     hidden = (gate * (1.0 / (1.0 + jnp.exp(-gate))) * (up_sum[...] * scale)).astype(jnp.bfloat16)
     weight[4].wait()
 
-    @pl.loop(0, chunks)
-    def _(chunk):
-        here = pl.ds(pl.multiple_of(chunk * CHUNK, CHUNK), CHUNK)
-        part = jnp.dot(hidden, w_down[:, here], preferred_element_type=jnp.float32)
-        for i in range(per_chunk):
-            part_f32[pl.ds(chunk * per_chunk + i, size, stride=tiles), :] = part[
-                :, i * LANES : (i + 1) * LANES
-            ]
-
-    @pl.loop(0, n)
-    def _(index):
-        here = pl.ds(pl.multiple_of(index * block, 16), block)
-        part_all[lax.rem(index, 2), index // 2] = part_f32[here, :].astype(jnp.bfloat16)
-
-    pair = pltpu.make_async_remote_copy(
-        src_ref=part_all.at[1 - core], dst_ref=pair_in, send_sem=pair_sem.at[0],
-        recv_sem=pair_sem.at[1], device_id={"tensor": partner}, device_id_type=MESH,
-    )
-    pair.start()
-    pair.wait_recv()
-
-    def summed(index):
-        return part_all[core, index].astype(jnp.float32) + pair_in[index].astype(jnp.float32)
-
-    def deliver(step):
-        target = chip_at(step)
-        return transfer(
-            3, pair_out.at[target], part_in.at[chip], target * 2 + core, send_sem.at[3, step], chip
-        )
-
-    @pl.loop(1, chips)
-    def _(step):
-        target = chip_at(chips - step)
-        pair_out[target] = summed(target).astype(jnp.bfloat16)
-        deliver(chips - step).start()
-
-    part_in[chip] = summed(chip).astype(jnp.bfloat16)
+    def pair(piece):
+        return pltpu.make_async_remote_copy(
+            src_ref=part_all.at[piece, 1 - core], dst_ref=pair_in.at[piece],
+            send_sem=pair_sem.at[0, piece], recv_sem=pair_sem.at[1, piece],
+            device_id={"tensor": partner}, device_id_type=MESH,
+        )
+
+    def summed(piece, index):
+        return (
+            part_all[piece, core, index].astype(jnp.float32)
+            + pair_in[piece, index].astype(jnp.float32)
+        )
+
+    def delivery(piece, target, slot, step):
+        return pltpu.make_async_remote_copy(
+            src_ref=pair_out.at[piece, target], dst_ref=part_in.at[piece, slot],
+            send_sem=out_send.at[piece, step], recv_sem=out_recv.at[piece, slot],
+            device_id={"tensor": target * 2 + core}, device_id_type=MESH,
+        )
+
+    strip = 4 * LANES
+    for piece in range(pieces):
+        for j in range(PIECE * LANES // strip):
+            first = piece * PIECE * LANES + j * strip
+            part = jnp.dot(
+                hidden, w_down[:, first : first + strip], preferred_element_type=jnp.float32
+            )
+            for i in range(strip // LANES):
+                part_f32[piece, pl.ds(j * (strip // LANES) + i, size, stride=PIECE), :] = part[
+                    :, i * LANES : (i + 1) * LANES
+                ]
+
+        @pl.loop(0, chips, unroll=4)
+        def _(index):
+            for c in range(2):
+                here = pl.ds(pl.multiple_of((index * 2 + c) * share, 16), share)
+                part_all[piece, c, index] = part_f32[piece, here, :].astype(jnp.bfloat16)
+
+        pair(piece).start()
+
+    for piece in range(pieces):
+        pair(piece).wait_recv()
+
+        @pl.loop(1, chips)
+        def _(step):
+            target = chip_at(chips - step)
+            pair_out[piece, target] = summed(piece, target).astype(jnp.bfloat16)
+            delivery(piece, target, chip, chips - step).start()
+
+        part_in[piece, chip] = summed(piece, chip).astype(jnp.bfloat16)
 
     picked = [
         [
@@ -327,35 +341,35 @@
     gather_left(0, tok_all)
     gather_left(1, heads)
     gather_left(2, att_all)
-    pair.wait_send()
-
-    @pl.loop(1, chips)
-    def _(step):
-        source = chip_from(step)
-        transfer(
-            3, part_in.at[source], part_in.at[source], partner, send_sem.at[3, 0], source
-        ).wait_recv()
-
     owners = chips // EXPERT_WINDOW
-    residual = tok_f32[my_block, :]
-    for row in range(rows):
-        total = residual[row * tiles : (row + 1) * tiles, :]
-        for e in range(EXPERT_WINDOW):
-            expert = jnp.zeros((tiles, LANES), jnp.float32)
-            for j in range(owners):
-                expert = expert + part_in[
-                    e * owners + j, row * tiles : (row + 1) * tiles, :
-                ].astype(jnp.float32)
-            total = total + picked[row][e] * expert
-        stage[row * tiles : (row + 1) * tiles, :] = total
+    for piece in range(pieces):
+        pair(piece).wait_send()
+
+        @pl.loop(1, chips)
+        def _(step):
+            delivery(piece, chip, chip_from(step), step).wait_recv()
+
+        for row in range(rows):
+            first = row * tiles + piece * PIECE
+            total = tok_f32[pl.ds(pl.multiple_of(me * block + first, 8), PIECE), :]
+            for e in range(EXPERT_WINDOW):
+                expert = jnp.zeros((PIECE, LANES), jnp.float32)
+                for j in range(owners):
+                    expert = expert + part_in[
+                        piece, e * owners + j, row * PIECE : (row + 1) * PIECE, :
+                    ].astype(jnp.float32)
+                total = total + picked[row][e] * expert
+            stage[first : first + PIECE, :] = total
+
     for tile in range(tiles):
         out[:, tile * LANES : (tile + 1) * LANES] = stage[
             pl.ds(tile, rows, stride=tiles), :
         ].astype(jnp.bfloat16)
 
-    @pl.loop(1, chips)
-    def _(step):
-        deliver(step).wait_send()
+    for piece in range(pieces):
+        @pl.loop(1, chips)
+        def _(step):
+            delivery(piece, chip_at(step), chip, step).wait_send()
 
 
 def on_device(
@@ -367,6 +381,8 @@
     tiles = width // LANES
     block = rows * tiles
     per_dev = w_qkv.shape[1] // HEAD_DIM
+    pieces = tiles // PIECE
+    share = rows * PIECE
     cosine, sine = rotation_tables(size)
     bf16, f32 = jnp.bfloat16, jnp.float32
     any_space = pl.BlockSpec(memory_space=pl.ANY)
@@ -396,17 +412,19 @@
             pltpu.VMEM((size, w_gate.shape[1]), f32),
             pltpu.VMEM((size, w_up.shape[1]), f32),
             pltpu.VMEM((size, LANES), f32),
-            pltpu.VMEM((n * block, LANES), f32),
-            pltpu.VMEM((2, n // 2, block, LANES), bf16),
-            pltpu.VMEM((n // 2, block, LANES), bf16),
-            pltpu.VMEM((n // 2, block, LANES), bf16),
-            pltpu.VMEM((n // 2, block, LANES), bf16),
+            pltpu.VMEM((pieces, n * share, LANES), f32),
+            pltpu.VMEM((pieces, 2, n // 2, share, LANES), bf16),
+            pltpu.VMEM((pieces, n // 2, share, LANES), bf16),
+            pltpu.VMEM((pieces, n // 2, share, LANES), bf16),
+            pltpu.VMEM((pieces, n // 2, share, LANES), bf16),
             pltpu.SemaphoreType.DMA((7,)),
             pltpu.SemaphoreType.DMA((5,)),
-            pltpu.SemaphoreType.DMA((4, n // 2)),
             pltpu.SemaphoreType.DMA((3, n // 2)),
-            pltpu.SemaphoreType.DMA((4, n)),
-            pltpu.SemaphoreType.DMA((2,)),
+            pltpu.SemaphoreType.DMA((3, n // 2)),
+            pltpu.SemaphoreType.DMA((3, n)),
+            pltpu.SemaphoreType.DMA((2, pieces)),
+            pltpu.SemaphoreType.DMA((pieces, n // 2)),
+            pltpu.SemaphoreType.DMA((pieces, n // 2)),
         ],
         compiler_params=pltpu.CompilerParams(
             collective_id=0, has_side_effects=True, vmem_limit_bytes=56 * 1024 * 1024

time: 47.9 us -> 45.7 us (0.954)
  Pallas kernels: 46.3 us -> 44.2 us
    pallas_call x1, Pallas kernels: 46.3 us -> 44.2 us  [on_device(): pl.pallas_call(functools.partial(kernel, n), out_shape=jax.ShapeDtypeStru...]
where the time goes in v4:
time: 45.7 us; the launch traced here: 45.6 us
  Pallas kernels  44.2 us (97%)
  local copies, waits for them, and re-layouts  1.36 us (3%)
    pallas_call x1, Pallas kernels, on_device(): pl.pallas_call(functools.partial(kernel, n), out_shape=jax.ShapeDtypeStru...  44.2 us
    unnamed x1, local copies, waits for them, and re-layouts  1.36 us

profile of v4, /device:TPU:0, one launch (start us, length us, event | category | flops | bytes accessed | tf_op | source)
XLA Modules:
  0.0 45.6 jit_solution(5271962074155301662)
XLA Ops:
  0.0 44.2 %layer.1 = bf16[2,6144]{1,0:T(2,128)(2,1)} custom-call(bf16[2,6144]{1,0:T(2,128)(2,1)} %tok_in.1, f32[48,128]{1,0:T(8,128)} %bitcast.2, bf16[6144,512]{1,0:T(8,128)(2,1)} %w_qkv_in.1, bf16[6144,384]{1,0:T(8,128)(2,1)} %w_out_in.1, f32[48,128]{1,0:T(8,128)} %bitcast.3, bf16[6144,256]{1,0:T(8,128)(2,1)} %w_gate_in.1, bf16[6144,256]{1,0:T(8,128)(2,1)} %w_up_in.1, ...), custom_call_target="tpu_custom_call" | custom-call | tf_op jit(solution)/shard_map/layer/pallas_call | solution.py:389
  44.2 1.4 %copy.14 = bf16[2,6144]{1,0:T(2,128)(2,1)} copy(bf16[2,6144]{1,0:T(2,128)(2,1)} %layer.1) | data formatting | bytes 49152

commit v5 on v4

--- a/solution.py
+++ b/solution.py
@@ -75,10 +75,7 @@
              (w_down_in, w_down)]
         )
     ]
-    for copy in small:
-        copy.start()
-    for copy in weight:
-        copy.start()
+    small[0].start()
 
     def chip_at(step):
         bits = [2**b for b in range(chips.bit_length() - 1)]
@@ -95,6 +92,10 @@
             barrier, inc=1, device_id={"tensor": chip_at(step) * 2 + core}, device_id_type=MESH
         )
 
+    for copy in small[1:]:
+        copy.start()
+    for copy in weight:
+        copy.start()
     small[0].wait()
     for tile in range(tiles):
         piece = own_tok[:, tile * LANES : (tile + 1) * LANES].astype(jnp.float32)

time: 45.7 us -> 45.3 us (level)
  Pallas kernels: 44.2 us -> 43.7 us
where the time goes in v5:
time: 45.3 us; the launch traced here: 45.1 us
  Pallas kernels  43.7 us (96%)
  local copies, waits for them, and re-layouts  1.36 us (3%)
    pallas_call x1, Pallas kernels, on_device(): pl.pallas_call(functools.partial(kernel, n), out_shape=jax.ShapeDtypeStru...  43.7 us
    unnamed x1, local copies, waits for them, and re-layouts  1.36 us

profile of v5, /device:TPU:0, one launch (start us, length us, event | category | flops | bytes accessed | tf_op | source)
XLA Modules:
  0.0 45.1 jit_solution(11199085277824640058)
XLA Ops:
  0.0 43.7 %layer.1 = bf16[2,6144]{1,0:T(2,128)(2,1)} custom-call(bf16[2,6144]{1,0:T(2,128)(2,1)} %tok_in.1, f32[48,128]{1,0:T(8,128)} %bitcast.2, bf16[6144,512]{1,0:T(8,128)(2,1)} %w_qkv_in.1, bf16[6144,384]{1,0:T(8,128)(2,1)} %w_out_in.1, f32[48,128]{1,0:T(8,128)} %bitcast.3, bf16[6144,256]{1,0:T(8,128)(2,1)} %w_gate_in.1, bf16[6144,256]{1,0:T(8,128)(2,1)} %w_up_in.1, ...), custom_call_target="tpu_custom_call" | custom-call | tf_op jit(solution)/shard_map/layer/pallas_call | solution.py:390
  43.8 1.4 %copy.14 = bf16[2,6144]{1,0:T(2,128)(2,1)} copy(bf16[2,6144]{1,0:T(2,128)(2,1)} %layer.1) | data formatting | bytes 49152
